TPU v7x, 32 devices: a whole 2x2x4 slice. The times are simulated.
32 devices in a mesh: dp: 4 (over y, x), table: 8 (over z, core).
Axes of the slice: x: 2, y: 2, z: 4, core: 2. Of those that a mesh axis runs over, the one named last changes fastest.
Arguments:
- item_ids: int32 [8192], P('dp'), may hold values from 0 to 32767
- user_len: int32 [32], P('dp'), may hold values from 32 to 256
- emb_table: bfloat16 [512, 32768], P('table'), may hold values from -6 to 6
- cotangent: bfloat16 [512, 8192], P('table', 'dp'), may hold values from -6 to 6
- w_uvqk: bfloat16 [512, 2048], replicated, may hold values from -0.25 to 0.25
- w_out: bfloat16 [512, 512], replicated, may hold values from -0.25 to 0.25
- gain_in: float32 [512], replicated, may hold values from 0.25 to 1.75
- gain_mid: float32 [512], replicated, may hold values from 0.25 to 1.75
Outputs:
- layer_out: bfloat16 [512, 8192], P('table', 'dp')
- table_grad: float32 [512, 32768], P('table', 'dp')
All inputs are finite; a program needn't handle non-finite values.
Results may differ from a plain program's by a relative error of at most 0.012.
Values may be sent and summed in bfloat16 or wider, within the bound.
No kernel may reach another device: no remote copies, remote signals or barrier semaphores. Data moves between devices by JAX's collectives and lax.ppermute only.
A program may use at most 128 MiB of HBM per device.

v0:
```python
import functools

import jax
import jax.numpy as jnp
from jax import lax
from jax.experimental import pallas as pl
from jax.experimental.pallas import tpu as pltpu
from jax.sharding import PartitionSpec as P

HEADS = 8
NORM_EPS = 1e-05
LANES = 128
WHOLE_VMEM_BYTES = 61 * 1024 * 1024
LAYER_VMEM_BYTES = 20 * 1024 * 1024
PLAN_VMEM_BYTES = 16 * 1024 * 1024
LIST_VMEM_BYTES = 24 * 1024 * 1024

F32 = jnp.float32
BF16 = jnp.bfloat16


def dot_nn(left, right):
    return jnp.dot(left, right, preferred_element_type=F32)


def dot_nt(left, right):
    return lax.dot_general(left, right, (((1,), (1,)), ((), ())), preferred_element_type=F32)


def dot_tn(left, right):
    return lax.dot_general(left, right, (((0,), (0,)), ((), ())), preferred_element_type=F32)


BLOCK = 256
UNROLL = 128
AT_ONCE = 32
CHUNKS = 4


def gather_kernel(
    len_ref,
    ids_ref,
    cot_hbm_ref,
    table_hbm_ref,
    out_ref,
    valid_ref,
    table_ref,
    cot_ref,
    rows_ref,
    picked_ref,
    turned_ref,
    row_vector_ref,
    row_ref,
    chunk_sems,
    row_sem,
    out_sems,
    cot_sems,
    cot_sem,
):
    users, _, positions = out_ref.shape
    features, vocab = table_hbm_ref.shape
    pack = LANES // features
    span = BLOCK * pack
    block_bits = BLOCK.bit_length() - 1

    def chunk_copy(chunk):
        columns = pl.ds(chunk * (vocab // CHUNKS), vocab // CHUNKS)
        return pltpu.make_async_copy(
            table_hbm_ref.at[:, columns], table_ref.at[:, columns], chunk_sems.at[chunk]
        )

    def cot_out_copy(user):
        return pltpu.make_async_copy(
            cot_ref.at[:, pl.ds(user * positions, positions)],
            out_ref.at[user, pl.ds(features, features), :],
            cot_sems.at[user],
        )

    def out_copy(user):
        return pltpu.make_async_copy(
            turned_ref.at[user], out_ref.at[user, pl.ds(0, features), :], out_sems.at[user]
        )

    for chunk in range(CHUNKS):
        chunk_copy(chunk).start()
    cot_copy = pltpu.make_async_copy(cot_hbm_ref, cot_ref, cot_sem)
    cot_copy.start()
    items = ids_ref[...]
    row_vector_ref[...] = ((items >> (span.bit_length() - 1)) << block_bits) | (items & (BLOCK - 1))
    row_copy = pltpu.make_async_copy(row_vector_ref, row_ref, row_sem)
    row_copy.start()
    order = lax.broadcasted_iota(jnp.int32, (1, positions), 1)
    for user in range(users):
        own_items = ids_ref[pl.ds(user * positions, positions)].reshape(1, positions)
        valid_ref[pl.ds(user, 1), :] = jnp.where(order < len_ref[user], own_items, vocab)

    parts = vocab // span
    for part in range(parts):
        if part % (parts // CHUNKS) == 0:
            chunk_copy(part // (parts // CHUNKS)).wait()
        stack = jnp.concatenate(
            [
                table_ref[:, part * span + s * BLOCK : part * span + (s + 1) * BLOCK]
                for s in range(pack)
            ],
            axis=0,
        )
        rows_ref[pl.ds(part * BLOCK, BLOCK), :] = stack.T.astype(F32)
    cot_copy.wait()
    for user in range(users):
        cot_out_copy(user).start()
    row_copy.wait()

    def some(part, carry):
        start = pl.multiple_of(part * UNROLL, UNROLL)
        for first in range(0, UNROLL, AT_ONCE):
            slots = range(first, first + AT_ONCE)
            rows = [rows_ref[pl.ds(row_ref[start + slot], 1), :] for slot in slots]
            for slot, row in zip(slots, rows):
                picked_ref[pl.ds(start + slot, 1), :] = row
        return carry

    lax.fori_loop(0, users * positions // UNROLL, some, 0)
    row = lax.broadcasted_iota(jnp.int32, (LANES, LANES), 0)
    column = lax.broadcasted_iota(jnp.int32, (LANES, LANES), 1)
    same = jnp.where(row == column, 1.0, 0.0).astype(BF16)
    for user in range(users):
        places = pl.ds(user * positions, positions)
        turned = dot_nt(same, picked_ref[places, :].astype(BF16))
        own_items = ids_ref[places].reshape(1, positions)
        group = (own_items >> block_bits) & (pack - 1)
        total = turned[:features]
        for s in range(1, pack):
            total = jnp.where(group == s, turned[s * features : (s + 1) * features], total)
        turned_ref[user] = total.astype(BF16)
        out_copy(user).start()
    for user in range(users):
        cot_out_copy(user).wait()
        out_copy(user).wait()


def gather_columns(item_ids, lengths, cotangent, table):
    users = lengths.shape[0]
    rows = item_ids.shape[0]
    positions = rows // users
    features, vocab = table.shape
    pack = LANES // features
    shape = (users, 2 * features, positions)
    hbm = pl.BlockSpec(memory_space=pltpu.HBM)
    vmem = pl.BlockSpec(memory_space=pltpu.VMEM)
    return pl.pallas_call(
        gather_kernel,
        out_shape=[
            jax.ShapeDtypeStruct(shape, table.dtype),
            jax.ShapeDtypeStruct((users, positions), jnp.int32),
        ],
        in_specs=[pl.BlockSpec(memory_space=pltpu.SMEM), vmem, hbm, hbm],
        out_specs=[hbm, vmem],
        scratch_shapes=[
            pltpu.VMEM((features, vocab), table.dtype),
            pltpu.VMEM((features, rows), table.dtype),
            pltpu.VMEM((vocab // pack, LANES), F32),
            pltpu.VMEM((rows, LANES), F32),
            pltpu.VMEM((users, features, positions), table.dtype),
            pltpu.VMEM((rows,), jnp.int32),
            pltpu.SMEM((rows,), jnp.int32),
            pltpu.SemaphoreType.DMA((CHUNKS,)),
            pltpu.SemaphoreType.DMA,
            pltpu.SemaphoreType.DMA((users,)),
            pltpu.SemaphoreType.DMA((users,)),
            pltpu.SemaphoreType.DMA,
        ],
        compiler_params=pltpu.CompilerParams(vmem_limit_bytes=WHOLE_VMEM_BYTES),
        cost_estimate=pl.CostEstimate(flops=8 * 10**9, bytes_accessed=5 * 10**6, transcendentals=0),
        name="gather_columns",
    )(lengths, item_ids, cotangent, table)


def norm_forward(values):
    centred = values - jnp.mean(values, axis=0, keepdims=True)
    inverse = lax.rsqrt(jnp.mean(centred * centred, axis=0, keepdims=True) + NORM_EPS)
    return centred * inverse, inverse


def norm_backward_means(grad, normal):
    return jnp.mean(grad, axis=0, keepdims=True), jnp.mean(grad * normal, axis=0, keepdims=True)


def norm_backward(grad, normal, inverse):
    shift, slope = norm_backward_means(grad, normal)
    return (grad - shift - normal * slope) * inverse


def silu_pair(half):
    turn = jnp.tanh(half)
    twice = 1.0 + turn
    value = half * twice
    return value, twice + value * (1.0 - turn)


def layer_kernel(
    me_ref,
    len_ref,
    recv_ref,
    w_in_ref,
    w_out_ref,
    gain_in_row_ref,
    gain_mid_row_ref,
    out_hbm_ref,
    grad_hbm_ref,
    out_ref,
    grad_ref,
    proj_ref,
    slope_ref,
    weight_ref,
    score_slope_ref,
    att_ref,
    dproj_ref,
    gain_in_ref,
    gain_mid_ref,
    share_ref,
    sems,
):
    peers, both, positions = recv_ref.shape
    features = both // 2
    width = peers * features
    head_dim = width // HEADS
    half = positions // 2

    out_copy = pltpu.make_async_copy(out_ref, out_hbm_ref, sems.at[0])

    def grad_copy(peer):
        rows = pl.ds(peer * features, features)
        return pltpu.make_async_copy(
            grad_ref.at[rows, :], grad_hbm_ref.at[rows, :], sems.at[1 + peer]
        )

    length = len_ref[me_ref[0]]
    share = 1.0 / length.astype(F32)
    for row_ref, column_ref in ((gain_in_row_ref, gain_in_ref), (gain_mid_row_ref, gain_mid_ref)):
        row = row_ref[...].reshape(1, width)
        tile = jnp.broadcast_to(row, (LANES, width)).T
        column_ref[...] = jnp.concatenate([tile] * (positions // LANES), axis=1)

    key = lax.broadcasted_iota(jnp.int32, (positions, positions), 0)
    query = lax.broadcasted_iota(jnp.int32, (positions, positions), 1)
    share_ref[...] = jnp.where((key <= query) & (key < length), share, 0.0)

    def joined(kind):
        rows = pl.ds(kind * features, features)
        return jnp.concatenate([recv_ref[peer, rows, :] for peer in range(peers)], axis=0)

    embedded = joined(0).astype(F32)
    normal_in, inverse_in = norm_forward(embedded)
    normed = (normal_in * gain_in_ref[...]).astype(BF16)

    def project(part):
        return dot_nn(w_in_ref[:, pl.ds(part * width, width)].T, normed)

    def store_projected(part, z):
        rows = pl.ds(part * width, width)
        value, slope = silu_pair(0.5 * z)
        proj_ref[rows, :] = value.astype(BF16)
        slope_ref[rows, :] = slope

    waiting = None
    for part in (2, 3, 1, 0):
        z = project(part)
        if waiting is not None:
            store_projected(*waiting)
        waiting = (part, z)
    store_projected(*waiting)

    starts = (0, half)
    scale = head_dim ** (-0.5)

    def head_rows(kind, head):
        return pl.ds(kind * width + head * head_dim, head_dim)

    def score(head):
        queries, keys = proj_ref[head_rows(2, head), :], proj_ref[head_rows(3, head), :]
        return [dot_tn(keys[:, start : start + half], queries[:, start:]) for start in starts]

    def store_weights(head, scores):
        for start, block in zip(starts, scores):
            value, slope = silu_pair(block * (0.5 * scale))
            places = (pl.ds(start, half), pl.ds(start, positions - start))
            weight_ref[head, *places] = (value * share_ref[*places]).astype(BF16)
            score_slope_ref[head, *places] = slope * share_ref[*places]
        weight_ref[head, pl.ds(half, half), pl.ds(0, half)] = jnp.zeros((half, half), BF16)

    def attend(head):
        att_ref[pl.ds(head * head_dim, head_dim), :] = dot_nn(
            proj_ref[head_rows(1, head), :], weight_ref[head]
        )

    scores = score(0)
    for head in range(HEADS):
        following = score(head + 1) if head + 1 < HEADS else None
        store_weights(head, scores)
        if head:
            attend(head - 1)
        scores = following
    attend(HEADS - 1)

    normal_mid, inverse_mid = norm_forward(att_ref[...])
    gate_rows = proj_ref[pl.ds(0, width), :].astype(F32)
    scaled = normal_mid * gain_mid_ref[...]
    mixed = (scaled * gate_rows).astype(BF16)
    valid = lax.broadcasted_iota(jnp.int32, (width, positions), 1) < length
    cotangent = jnp.where(valid, joined(1).astype(F32), 0.0)
    d_mixed = dot_nn(w_out_ref[...], cotangent.astype(BF16))
    out_ref[...] = (embedded + dot_nn(w_out_ref[...].T, mixed)).astype(BF16)
    out_copy.start()

    dproj_ref[pl.ds(0, width), :] = (d_mixed * scaled * slope_ref[pl.ds(0, width), :]).astype(BF16)
    d_att = norm_backward(d_mixed * gate_rows * gain_mid_ref[...], normal_mid, inverse_mid)
    att_ref[...] = d_att

    def d_weights(head):
        values = proj_ref[head_rows(1, head), :]
        d_head = att_ref[pl.ds(head * head_dim, head_dim), :].astype(BF16)
        return [dot_tn(values[:, start : start + half], d_head[:, start:]) for start in starts]

    def d_scores(head, products):
        low, high = (
            (block * score_slope_ref[head, pl.ds(start, half), pl.ds(start, positions - start)]).astype(
                BF16
            )
            for start, block in zip(starts, products)
        )
        empty = jnp.zeros((half, half), BF16)
        return jnp.concatenate([low, jnp.concatenate([empty, high], axis=1)], axis=0)

    def d_project(head, d_score):
        d_head = att_ref[pl.ds(head * head_dim, head_dim), :].astype(BF16)
        queries, keys = proj_ref[head_rows(2, head), :], proj_ref[head_rows(3, head), :]
        products = (
            dot_nt(d_head, weight_ref[head]),
            dot_nn(keys, d_score) * (0.5 * scale),
            dot_nt(queries, d_score) * (0.5 * scale),
        )
        for kind, product in zip((1, 2, 3), products):
            rows = head_rows(kind, head)
            dproj_ref[rows, :] = (product * slope_ref[rows, :]).astype(BF16)

    products, before = d_weights(0), None
    for head in range(HEADS):
        following = d_weights(head + 1) if head + 1 < HEADS else None
        d_score = d_scores(head, products)
        if head:
            d_project(head - 1, before)
        products, before = following, d_score
    d_project(HEADS - 1, before)

    d_normed = dot_nn(w_in_ref[...], dproj_ref[...])
    d_normal = d_normed * (0.5 * gain_in_ref[...])
    shift, slope = norm_backward_means(d_normal, normal_in)
    for peer in range(peers):
        rows = slice(peer * features, (peer + 1) * features)
        d_embedded = (d_normal[rows] - shift - normal_in[rows] * slope) * inverse_in
        grad_ref[rows, :] = (cotangent[rows] + d_embedded).astype(BF16)
        grad_copy(peer).start()
    out_copy.wait()
    for peer in range(peers):
        grad_copy(peer).wait()


def run_layer(me, lengths, received, w_in, w_out, gain_in, gain_mid):
    peers, _, positions = received.shape
    width = w_out.shape[0]
    smem, vmem = pl.BlockSpec(memory_space=pltpu.SMEM), pl.BlockSpec(memory_space=pltpu.VMEM)
    hbm = pl.BlockSpec(memory_space=pltpu.HBM)
    shape = jax.ShapeDtypeStruct((width, positions), BF16)
    return pl.pallas_call(
        layer_kernel,
        out_shape=[shape, shape],
        in_specs=[smem, smem] + [vmem] * 5,
        out_specs=[hbm, hbm],
        scratch_shapes=[
            pltpu.VMEM((width, positions), BF16),
            pltpu.VMEM((width, positions), BF16),
            pltpu.VMEM((4 * width, positions), BF16),
            pltpu.VMEM((4 * width, positions), F32),
            pltpu.VMEM((HEADS, positions, positions), BF16),
            pltpu.VMEM((HEADS, positions, positions), F32),
            pltpu.VMEM((width, positions), F32),
            pltpu.VMEM((4 * width, positions), BF16),
            pltpu.VMEM((width, positions), F32),
            pltpu.VMEM((width, positions), F32),
            pltpu.VMEM((positions, positions), F32),
            pltpu.SemaphoreType.DMA((1 + peers,)),
        ],
        compiler_params=pltpu.CompilerParams(vmem_limit_bytes=LAYER_VMEM_BYTES),
        cost_estimate=pl.CostEstimate(flops=10**10, bytes_accessed=10**7, transcendentals=10**6),
        name="layer",
    )(
        me,
        lengths,
        received,
        w_in,
        w_out,
        gain_in,
        gain_mid,
    )


LOW = 256
STACK = 16


def ranks(member, users):
    rows, positions = member.shape
    ones = jnp.where(member, 1.0, 0.0).astype(BF16)

    def iota(shape, dimension):
        return lax.broadcasted_iota(jnp.int32, shape, dimension)

    square = (positions, positions)
    before = jnp.where(iota(square, 0) < iota(square, 1), 1.0, 0.0).astype(BF16)
    row, other = iota((rows, rows), 0), iota((rows, rows), 1)
    shift = users.bit_length() - 1
    above = (other < row) & ((other >> shift) == (row >> shift))
    earlier = dot_nn(jnp.where(above, 1.0, 0.0).astype(BF16), ones)
    return (dot_nn(ones, before) + jnp.sum(earlier, axis=1, keepdims=True)).astype(jnp.int32)


def plan_kernel(own, home_ref, turn_ref, ids_ref, low_ref, high_ref, slot_ref, most_ref, *scratch):
    chosen_ref, digit_ref, wide_ref, rank_ref = scratch
    groups, users, positions = ids_ref.shape
    capacity = low_ref.shape[1]
    home = home_ref[0]
    first = turn_ref[0] * capacity
    own_bits, low_bits = own.bit_length() - 1, LOW.bit_length() - 1

    all_items = ids_ref[...].reshape(groups * users, positions)
    sent = jnp.concatenate([ids_ref[0] >> own_bits == owner for owner in range(groups)], axis=0)
    arriving = all_items >> own_bits == home
    rank_ref[...] = ranks(jnp.concatenate([arriving, sent], axis=0), users) - first
    slot = jnp.full((users, positions), -1, jnp.int32)
    for owner in range(groups):
        rank = rank_ref[pl.ds((groups + owner) * users, users), :]
        fits = (ids_ref[0] >> own_bits == owner) & (rank >= 0) & (rank < capacity)
        slot = jnp.where(fits, rank + owner * capacity, slot)
    slot_ref[...] = slot

    digit = lax.broadcasted_iota(jnp.int32, (LOW, positions), 0)
    place = lax.broadcasted_iota(jnp.int32, (capacity, positions), 0)

    def one_group(group, most):
        items = ids_ref[group]
        for owner in range(groups):
            count = jnp.sum(jnp.where(items >> own_bits == owner, 1.0, 0.0))
            most = jnp.maximum(most, count)
        mine = items >> own_bits == home
        local = items & (own - 1)
        rank = rank_ref[pl.ds(pl.multiple_of(group * users, users), users), :]
        slot = jnp.where(mine, rank, -1)
        low = local & (LOW - 1)
        high = jnp.where(mine, (local >> low_bits) + 1, 0).astype(F32)
        for user in range(users):
            columns = pl.ds(user * positions, positions)
            chosen_ref[:, columns] = jnp.where(place == slot[user : user + 1], 1.0, 0.0).astype(BF16)
            digit_ref[:, columns] = jnp.where(digit == low[user : user + 1], 1.0, 0.0).astype(BF16)
            wide_ref[:, columns] = jnp.broadcast_to(high[user : user + 1], (16, positions)).astype(BF16)
        low_ref[group] = dot_nt(chosen_ref[...], digit_ref[...]).astype(BF16)
        high_ref[pl.ds(group, 1), :] = dot_nt(wide_ref[...], chosen_ref[...])[:1]
        return most

    most_ref[0] = lax.fori_loop(0, groups, one_group, jnp.float32(0)).astype(jnp.int32)


def plan_turn(home, turn, all_ids, own, capacity):
    groups, users, positions = all_ids.shape
    smem, vmem = pl.BlockSpec(memory_space=pltpu.SMEM), pl.BlockSpec(memory_space=pltpu.VMEM)
    return pl.pallas_call(
        functools.partial(plan_kernel, own),
        out_shape=[
            jax.ShapeDtypeStruct((groups, capacity, LOW), BF16),
            jax.ShapeDtypeStruct((groups, capacity), F32),
            jax.ShapeDtypeStruct((users, positions), jnp.int32),
            jax.ShapeDtypeStruct((1,), jnp.int32),
        ],
        in_specs=[smem, smem, vmem],
        out_specs=[vmem] * 3 + [smem],
        scratch_shapes=[
            pltpu.VMEM((capacity, users * positions), BF16),
            pltpu.VMEM((LOW, users * positions), BF16),
            pltpu.VMEM((16, users * positions), BF16),
            pltpu.VMEM((2 * groups * users, positions), jnp.int32),
        ],
        compiler_params=pltpu.CompilerParams(vmem_limit_bytes=PLAN_VMEM_BYTES),
        cost_estimate=pl.CostEstimate(flops=4 * 10**9, bytes_accessed=5 * 10**6, transcendentals=0),
        name="plan_turn",
    )(home, turn, all_ids)


def pack_kernel(distances, home_ref, slot_ref, grad_ref, *refs):
    *packed_refs, wide_ref, chosen_ref = refs
    users, _, positions = grad_ref.shape
    capacity = packed_refs[0].shape[1]
    padded = jnp.concatenate(
        [slot_ref[...].astype(F32), jnp.zeros((LANES - users, positions), F32)], axis=0
    )
    slots = padded.T.astype(jnp.int32)
    place = lax.broadcasted_iota(jnp.int32, (positions, capacity), 1)
    for user in range(users):
        wide_ref[:, pl.ds(user * positions, positions)] = grad_ref[user]
    for distance, packed_ref in zip(distances, packed_refs):
        first = (home_ref[0] ^ distance) * capacity
        for user in range(users):
            chosen_ref[pl.ds(user * positions, positions), :] = jnp.where(
                place == slots[:, user : user + 1] - first, 1.0, 0.0
            ).astype(BF16)
        packed_ref[...] = dot_nn(wide_ref[...], chosen_ref[...]).astype(BF16)


def pack_lists(distances, home, slot, grads, capacity):
    users, features, positions = grads.shape
    smem, vmem = pl.BlockSpec(memory_space=pltpu.SMEM), pl.BlockSpec(memory_space=pltpu.VMEM)
    return pl.pallas_call(
        functools.partial(pack_kernel, distances),
        out_shape=[jax.ShapeDtypeStruct((features, capacity), BF16)] * len(distances),
        in_specs=[smem, vmem, vmem],
        out_specs=[vmem] * len(distances),
        scratch_shapes=[
            pltpu.VMEM((features, users * positions), BF16),
            pltpu.VMEM((users * positions, capacity), BF16),
        ],
        compiler_params=pltpu.CompilerParams(vmem_limit_bytes=LIST_VMEM_BYTES),
        cost_estimate=pl.CostEstimate(
            flops=len(distances) * 8 * 10**8, bytes_accessed=10**6, transcendentals=0
        ),
        name="pack_lists",
    )(home, slot, grads)


def scatter_kernel(groups, stack, low_ref, high_ref, *refs):
    list_refs, (*before_ref, out_ref, spread_ref) = refs[:groups], refs[groups:]
    features, capacity = list_refs[0].shape
    step = pl.program_id(0)
    for group, list_ref in enumerate(list_refs):
        high = high_ref[pl.ds(group, 1), :]
        for part in range(stack):
            wanted = (step * stack + part + 1).astype(F32)
            chosen = jnp.where(high == wanted, 1.0, 0.0).astype(BF16)
            spread_ref[pl.ds(part * features, features), pl.ds(group * capacity, capacity)] = (
                list_ref[...] * chosen
            )
    sums = dot_nn(spread_ref[...], low_ref[...])
    for part in range(stack):
        columns = pl.ds(part * LOW, LOW)
        term = sums[part * features : (part + 1) * features]
        out_ref[:, columns] = term + before_ref[0][:, columns] if before_ref else term


def scatter_slots(low, high, lists, own, before=None):
    groups = len(lists)
    features, capacity = lists[0].shape
    low = low.reshape(groups * capacity, LOW)
    stack = min(STACK, own // LOW)
    block = pl.BlockSpec((features, stack * LOW), lambda i: (0, i))
    extra = [] if before is None else [before]
    return pl.pallas_call(
        functools.partial(scatter_kernel, groups, stack),
        grid=(own // (LOW * stack),),
        out_shape=jax.ShapeDtypeStruct((features, own), F32),
        in_specs=[
            pl.BlockSpec((groups * capacity, LOW), lambda i: (0, 0)),
            pl.BlockSpec(high.shape, lambda i: (0, 0)),
        ]
        + [pl.BlockSpec((features, capacity), lambda i: (0, 0))] * groups
        + [block] * len(extra),
        out_specs=block,
        scratch_shapes=[pltpu.VMEM((stack * features, groups * capacity), BF16)],
        input_output_aliases={2 + groups: 0} if extra else {},
        compiler_params=pltpu.CompilerParams(vmem_limit_bytes=LIST_VMEM_BYTES),
        cost_estimate=pl.CostEstimate(flops=3 * 10**9, bytes_accessed=10**6, transcendentals=0),
        name="scatter_slots",
    )(low, high, *lists, *extra)


def swap(value, axis, distance):
    size = lax.axis_size(axis)
    return lax.ppermute(value, axis, [(i, i ^ distance) for i in range(size)])


def send_lists(home, slot, grads, owners, capacity):
    lists = [None] * owners
    for distances in ((owners - 1,), tuple(range(1, owners - 1)), (0,)):
        made = pack_lists(distances, home, slot, grads, capacity)
        slot, made = lax.optimization_barrier((slot, made))
        for distance, one_list in zip(distances, made):
            lists[distance] = swap(one_list, "dp", distance) if distance else one_list
    return lists


def exchange(value, axis):
    return lax.all_to_all(value, axis, split_axis=0, concat_axis=0, tiled=True)


def on_device(item_ids, user_len, emb_table, cotangent, w_uvqk, w_out, gain_in, gain_mid):
    dp_size = lax.axis_size("dp")
    table_size = lax.axis_size("table")
    users = user_len.shape[0]
    features, vocab = emb_table.shape
    rows = item_ids.shape[0]
    positions = rows // users
    own = vocab // dp_size
    capacity = -(-(rows // dp_size * 5 // 4) // LANES) * LANES
    assert users == table_size and users <= LANES and positions <= 256 and own // LOW <= 255
    assert dp_size & (dp_size - 1) == 0 and users & (users - 1) == 0 and own & (own - 1) == 0
    me = lax.axis_index("table").astype(jnp.int32).reshape(1)
    home = lax.axis_index("dp").astype(jnp.int32).reshape(1)

    send, valid_ids = gather_columns(item_ids, user_len, cotangent, emb_table)
    received = exchange(send, "table")
    all_ids = jnp.stack([valid_ids] + [swap(valid_ids, "dp", k) for k in range(1, dp_size)])
    out_cols, grad_cols = run_layer(me, user_len, received, w_uvqk, w_out, gain_in, gain_mid)
    per_peer = (table_size, features, positions)
    all_ids, grad_cols = lax.optimization_barrier((all_ids, grad_cols))
    plan = plan_turn(home, jnp.zeros((1,), jnp.int32), all_ids, own, capacity)
    grad_home = exchange(grad_cols.reshape(per_peer), "table")
    out_cols, grad_home, plan = lax.optimization_barrier((out_cols, grad_home, plan))
    out_home = exchange(out_cols.reshape(per_peer), "table")
    low, high, slot, most = plan
    lists = send_lists(home, slot, grad_home, dp_size, capacity)
    own_list, out_home = lax.optimization_barrier((lists[0], out_home))
    lists = [own_list] + lists[1:]
    layer_out = jnp.transpose(out_home, (1, 0, 2)).reshape(features, rows)
    layer_out, lists = lax.optimization_barrier((layer_out, lists))
    table_grad = scatter_slots(low, high, lists, own)

    turns = (most[0] + capacity - 1) // capacity

    def another(state):
        turn, sums = state
        more_low, more_high, more_slot, _ = plan_turn(home, turn.reshape(1), all_ids, own, capacity)
        more_lists = send_lists(home, more_slot, grad_home, dp_size, capacity)
        return turn + 1, scatter_slots(more_low, more_high, more_lists, own, sums)

    _, table_grad = lax.while_loop(
        lambda state: state[0] < turns, another, (jnp.int32(1), table_grad)
    )
    return (layer_out, table_grad)


def solution(mesh):
    return jax.shard_map(
        on_device,
        mesh=mesh,
        in_specs=(P("dp"), P("dp"), P("table", None), P("table", "dp"), P(), P(), P(), P()),
        out_specs=(P("table", "dp"), P("table", "dp")),
        check_vma=False,
    )
```

profile of v0, /device:TPU:0, one launch (start us, length us, event | category | flops | bytes accessed | tf_op | source)
XLA Modules:
  0.0 67.2 jit_solution(11592218823438759201)
XLA Ops:
  0.6 0.0 copy-start.4
  0.6 0.0 copy-start.3
  0.7 0.0 copy-start.2
  0.7 0.0 copy-start.1
  0.7 0.0 copy-start
  0.7 6.8 %gather_columns.1 = (bf16[8,128,256]{2,1,0:T(8,128)(2,1)}, s32[8,256]{1,0:T(8,128)}) custom-call(s32[8]{0:T(128)} %len_ref.3, s32[2048]{0:T(1024)} %ids_ref.1, bf16[64,2048]{1,0:T(8,128)(2,1)} %cot_hbm_ref.1, bf16[64,32768]{1,0:T(8,128)(2,1)} %table_hbm_ref.1), custom_call_target="tpu_custom_call" | custom-call | flops 8000000000 | bytes 5000000 | tf_op jit(solution)/shard_map/gather_columns/pallas_call | solution.py:151
  7.5 6.3 %all-to-all-start = ((bf16[8,128,256]{2,1,0:T(8,128)(2,1)}), bf16[8,128,256]{2,1,0:T(8,128)(2,1)S(1)}, u32[]{:S(2)}, u32[]{:S(2)}) async-start(bf16[8,128,256]{2,1,0:T(8,128)(2,1)} %get-tuple-element.77), calls=%async_computation | async-start | bytes 1048576 | tf_op jit(solution)/shard_map/all_to_all | solution.py:599
  13.8 2.4 %collective-permute-start.5 = (s32[8,256]{1,0:T(8,128)}, s32[8,256]{1,0:T(8,128)S(1)}, u32[]{:S(2)}, u32[]{:S(2)}) collective-permute-start(s32[8,256]{1,0:T(8,128)} %get-tuple-element.79), channel_id=1, source_target_pairs={{0,24},{8,16},{16,8},{24,0},{1,25},{9,17},{17,9},{25,1},{2,26},{10... | collective-permute-start | bytes 24584 | tf_op jit(solution)/shard_map/ppermute | solution.py:585
  16.3 0.5 collective-permute-start.4
  16.8 0.5 collective-permute-start.3
  17.3 1.3 %collective-permute-done.5 = s32[8,256]{1,0:T(8,128)S(1)} collective-permute-done((s32[8,256]{1,0:T(8,128)}, s32[8,256]{1,0:T(8,128)S(1)}, u32[]{:S(2)}, u32[]{:S(2)}) %collective-permute-start.5) | collective-permute-done | bytes 8224 | tf_op jit(solution)/shard_map/ppermute | solution.py:585
  18.6 1.5 %collective-permute-done.4 = s32[8,256]{1,0:T(8,128)S(1)} collective-permute-done((s32[8,256]{1,0:T(8,128)}, s32[8,256]{1,0:T(8,128)S(1)}, u32[]{:S(2)}, u32[]{:S(2)}) %collective-permute-start.4) | collective-permute-done | bytes 8224 | tf_op jit(solution)/shard_map/ppermute | solution.py:585
  20.1 0.5 collective-permute-done.3
  20.7 0.7 %pad_add_fusion.ids_ref = s32[4,8,256]{2,1,0:T(8,128)S(1)} fusion(s32[1,8,256]{2,1,0:T(8,128)S(1)} %bitcast.25, s32[1,8,256]{2,1,0:T(8,128)S(1)} %bitcast.26, s32[1,8,256]{2,1,0:T(8,128)S(1)} %bitcast.27, s32[1,8,256]{2,1,0:T(8,128)} %bitcast.24), kind=kLoop, calls=%fused_computation | loop fusion | flops 24576 | bytes 65536 | tf_op jit(solution)/shard_map/stack | solution.py:618
  21.4 7.8 %all-to-all-done.recv_ref = bf16[8,128,256]{2,1,0:T(8,128)(2,1)S(1)} async-done(((bf16[8,128,256]{2,1,0:T(8,128)(2,1)}), bf16[8,128,256]{2,1,0:T(8,128)(2,1)S(1)}, u32[]{:S(2)}, u32[]{:S(2)}) %all-to-all-start) | async-done | bytes 524320 | tf_op jit(solution)/shard_map/all_to_all | solution.py:599
  29.2 0.0 copy-done.4
  29.2 0.0 copy-done.3
  29.2 0.0 copy-done.2
  29.2 0.0 copy-done.1
  29.2 0.0 copy-done
  29.2 6.6 %layer.1 = (bf16[512,256]{1,0:T(8,128)(2,1)}, bf16[512,256]{1,0:T(8,128)(2,1)}) custom-call(s32[1]{0:T(128)} %bitcast.2.me_ref, s32[8]{0:T(128)S(1)} %copy-done.4, bf16[8,128,256]{2,1,0:T(8,128)(2,1)S(1)} %all-to-all-done.recv_ref, bf16[512,2048]{1,0:T(8,128)(2,1)S(1)} %copy-done, bf16[512,512]{1,0:T(8,128)(2,1)S(1)} %copy-done.1, f32[512]{0:T(512)S(1)} %copy-done.2, ...), custom_call_target="tpu_custom_call" | custom-call | flops 10000000000 | bytes 10000000 | tf_op jit(solution)/shard_map/layer/pallas_call | solution.py:375
  35.9 3.4 %all-to-all-start.1 = ((bf16[8,64,256]{2,1,0:T(8,128)(2,1)}), bf16[8,64,256]{2,1,0:T(8,128)(2,1)S(1)}, u32[]{:S(2)}, u32[]{:S(2)}) async-start(bf16[8,64,256]{2,1,0:T(8,128)(2,1)} %bitcast.7), calls=%async_computation.1 | async-start | bytes 524288 | tf_op jit(solution)/shard_map/all_to_all | solution.py:599
  39.3 6.9 %plan_turn.2 = (bf16[4,640,256]{2,1,0:T(8,128)(2,1)S(1)}, f32[4,640]{1,0:T(4,128)S(1)}, s32[8,256]{1,0:T(8,128)S(1)}, s32[1]{0:T(128)}) custom-call(s32[1]{0:T(128)} %bitcast.8.home_ref, s32[1]{0:T(128)} %constant.26.clone.1.turn_ref, s32[4,8,256]{2,1,0:T(8,128)S(1)} %pad_add_fusion.ids_ref), custom_call_target="tpu_custom_call" | custom-call | flops 4000000000 | bytes 5000000 | tf_op jit(solution)/shard_map/plan_turn/pallas_call | solution.py:476
  46.2 2.7 %all-to-all-done.1.grad_ref = bf16[8,64,256]{2,1,0:T(8,128)(2,1)S(1)} async-done(((bf16[8,64,256]{2,1,0:T(8,128)(2,1)}), bf16[8,64,256]{2,1,0:T(8,128)(2,1)S(1)}, u32[]{:S(2)}, u32[]{:S(2)}) %all-to-all-start.1) | async-done | bytes 262176 | tf_op jit(solution)/shard_map/all_to_all | solution.py:599
  48.9 3.6 %all-to-all-start.2 = ((bf16[8,64,256]{2,1,0:T(8,128)(2,1)}), bf16[8,64,256]{2,1,0:T(8,128)(2,1)S(1)}, u32[]{:S(2)}, u32[]{:S(2)}) async-start(bf16[8,64,256]{2,1,0:T(8,128)(2,1)} %bitcast.9), calls=%async_computation.2 | async-start | bytes 524288 | tf_op jit(solution)/shard_map/all_to_all | solution.py:599
  52.6 1.1 %pack_lists.6 = bf16[64,640]{1,0:T(8,128)(2,1)S(1)} custom-call(s32[1]{0:T(128)} %bitcast.8.home_ref, s32[8,256]{1,0:T(8,128)S(1)} %get-tuple-element.92.slot_ref, bf16[8,64,256]{2,1,0:T(8,128)(2,1)S(1)} %all-to-all-done.1.grad_ref), custom_call_target="tpu_custom_call" | custom-call | flops 800000000 | bytes 1000000 | tf_op jit(solution)/shard_map/pack_lists/pallas_call | solution.py:521
  53.7 2.5 %collective-permute-start.8 = (bf16[64,640]{1,0:T(8,128)(2,1)S(1)}, bf16[64,640]{1,0:T(8,128)(2,1)S(1)}, u32[]{:S(2)}, u32[]{:S(2)}) collective-permute-start(bf16[64,640]{1,0:T(8,128)(2,1)S(1)} %pack_lists.6), channel_id=1, source_target_pairs={{0,24},{8,16},{16,8},{24,0},{1,25},{9,17},{17,9},{25,1},{2,26},{10... | collective-permute-start | bytes 245768 | tf_op jit(solution)/shard_map/ppermute | solution.py:585
  56.2 1.9 %pack_lists.7 = (bf16[64,640]{1,0:T(8,128)(2,1)S(1)}, bf16[64,640]{1,0:T(8,128)(2,1)S(1)}) custom-call(s32[1]{0:T(128)} %bitcast.8.home_ref, s32[8,256]{1,0:T(8,128)S(1)} %get-tuple-element.92.slot_ref, bf16[8,64,256]{2,1,0:T(8,128)(2,1)S(1)} %all-to-all-done.1.grad_ref), custom_call_target="tpu_custom_call" | custom-call | flops 1600000000 | bytes 1000000 | tf_op jit(solution)/shard_map/pack_lists/pallas_call | solution.py:521
  58.1 0.6 collective-permute-start.6
  58.7 0.5 collective-permute-start.7
  59.9 1.1 %pack_lists.8.refs_0_ = bf16[64,640]{1,0:T(8,128)(2,1)S(1)} custom-call(s32[1]{0:T(128)} %bitcast.8.home_ref, s32[8,256]{1,0:T(8,128)S(1)} %get-tuple-element.92.slot_ref, bf16[8,64,256]{2,1,0:T(8,128)(2,1)S(1)} %all-to-all-done.1.grad_ref), custom_call_target="tpu_custom_call" | custom-call | flops 800000000 | bytes 1000000 | tf_op jit(solution)/shard_map/pack_lists/pallas_call | solution.py:521
  61.0 1.0 %all-to-all-done.2 = bf16[8,64,256]{2,1,0:T(8,128)(2,1)S(1)} async-done(((bf16[8,64,256]{2,1,0:T(8,128)(2,1)}), bf16[8,64,256]{2,1,0:T(8,128)(2,1)S(1)}, u32[]{:S(2)}, u32[]{:S(2)}) %all-to-all-start.2) | async-done | bytes 262176 | tf_op jit(solution)/shard_map/all_to_all | solution.py:599
  62.0 0.7 %copy.12 = bf16[8,8,8,256]{3,2,0,1:T(8,128)(2,1)} copy(bf16[8,8,8,256]{3,2,1,0:T(8,128)(2,1)S(1)} %bitcast.22) | data formatting | bytes 524288 | tf_op jit(solution)/shard_map/reshape | solution.py:630
  62.8 0.0 collective-permute-done.8.refs_3_
  62.8 0.0 collective-permute-done.6.refs_1_
  62.8 0.4 collective-permute-done.7.refs_2_
  63.1 4.0 %scatter_slots.2 = f32[64,8192]{1,0:T(8,128)} custom-call(bf16[2560,256]{1,0:T(8,128)(2,1)S(1)} %bitcast.20, f32[4,640]{1,0:T(4,128)S(1)} %get-tuple-element.102.high_ref, bf16[64,640]{1,0:T(8,128)(2,1)S(1)} %pack_lists.8.refs_0_, bf16[64,640]{1,0:T(8,128)(2,1)S(1)} %collective-permute-done.6.refs_1_, bf16[64,640]{1,0:T(8,128)(2,1)S(1)} %collective-permute-done.7.refs_2_, ...), custom_call_target="tpu_custom_call" | custom-call | flops 3000000000 | bytes 1000000 | tf_op jit(solution)/shard_map/scatter_slots/pallas_call | solution.py:564
  (1 shorter events, 0.0 us)
Async XLA Ops:
  0.6 28.6 %copy-start.4 = (s32[8]{0:T(128)S(1)}, s32[8]{0:T(128)}, u32[]{:S(2)}) copy-start(s32[8]{0:T(128)} %len_ref.3) | copy-start | bytes 100
  0.6 28.6 %copy-start.3 = (f32[512]{0:T(512)S(1)}, f32[512]{0:T(512)}, u32[]{:S(2)}) copy-start(f32[512]{0:T(512)} %gain_mid_row_ref.1) | copy-start | bytes 6148
  0.7 28.6 %copy-start.2 = (f32[512]{0:T(512)S(1)}, f32[512]{0:T(512)}, u32[]{:S(2)}) copy-start(f32[512]{0:T(512)} %gain_in_row_ref.1) | copy-start | bytes 6148
  0.7 28.5 %copy-start.1 = (bf16[512,512]{1,0:T(8,128)(2,1)S(1)}, bf16[512,512]{1,0:T(8,128)(2,1)}, u32[]{:S(2)}) copy-start(bf16[512,512]{1,0:T(8,128)(2,1)} %w_out_ref.1) | copy-start | bytes 1572868
  0.7 28.5 %copy-start = (bf16[512,2048]{1,0:T(8,128)(2,1)S(1)}, bf16[512,2048]{1,0:T(8,128)(2,1)}, u32[]{:S(2)}) copy-start(bf16[512,2048]{1,0:T(8,128)(2,1)} %w_in_ref.1) | copy-start | bytes 6291460
  7.5 21.7 %all-to-all-start = ((bf16[8,128,256]{2,1,0:T(8,128)(2,1)}), bf16[8,128,256]{2,1,0:T(8,128)(2,1)S(1)}, u32[]{:S(2)}, u32[]{:S(2)}) async-start(bf16[8,128,256]{2,1,0:T(8,128)(2,1)} %get-tuple-element.77), calls=%async_computation | async-start | bytes 1048576 | tf_op jit(solution)/shard_map/all_to_all | solution.py:599
  13.8 4.8 %collective-permute-start.5 = (s32[8,256]{1,0:T(8,128)}, s32[8,256]{1,0:T(8,128)S(1)}, u32[]{:S(2)}, u32[]{:S(2)}) collective-permute-start(s32[8,256]{1,0:T(8,128)} %get-tuple-element.79), channel_id=1, source_target_pairs={{0,24},{8,16},{16,8},{24,0},{1,25},{9,17},{17,9},{25,1},{2,26},{10... | collective-permute-start | bytes 24584 | tf_op jit(solution)/shard_map/ppermute | solution.py:585
  16.3 3.9 %collective-permute-start.4 = (s32[8,256]{1,0:T(8,128)}, s32[8,256]{1,0:T(8,128)S(1)}, u32[]{:S(2)}, u32[]{:S(2)}) collective-permute-start(s32[8,256]{1,0:T(8,128)} %get-tuple-element.79), channel_id=1, source_target_pairs={{0,16},{8,24},{16,0},{24,8},{1,17},{9,25},{17,1},{25,9},{2,18},{10... | collective-permute-start | bytes 24584 | tf_op jit(solution)/shard_map/ppermute | solution.py:585
  16.8 3.9 %collective-permute-start.3 = (s32[8,256]{1,0:T(8,128)}, s32[8,256]{1,0:T(8,128)S(1)}, u32[]{:S(2)}, u32[]{:S(2)}) collective-permute-start(s32[8,256]{1,0:T(8,128)} %get-tuple-element.79), channel_id=1, source_target_pairs={{0,8},{8,0},{16,24},{24,16},{1,9},{9,1},{17,25},{25,17},{2,10},{10... | collective-permute-start | bytes 24584 | tf_op jit(solution)/shard_map/ppermute | solution.py:585
  35.9 13.1 %all-to-all-start.1 = ((bf16[8,64,256]{2,1,0:T(8,128)(2,1)}), bf16[8,64,256]{2,1,0:T(8,128)(2,1)S(1)}, u32[]{:S(2)}, u32[]{:S(2)}) async-start(bf16[8,64,256]{2,1,0:T(8,128)(2,1)} %bitcast.7), calls=%async_computation.1 | async-start | bytes 524288 | tf_op jit(solution)/shard_map/all_to_all | solution.py:599
  48.9 13.1 %all-to-all-start.2 = ((bf16[8,64,256]{2,1,0:T(8,128)(2,1)}), bf16[8,64,256]{2,1,0:T(8,128)(2,1)S(1)}, u32[]{:S(2)}, u32[]{:S(2)}) async-start(bf16[8,64,256]{2,1,0:T(8,128)(2,1)} %bitcast.9), calls=%async_computation.2 | async-start | bytes 524288 | tf_op jit(solution)/shard_map/all_to_all | solution.py:599
  53.7 9.1 %collective-permute-start.8 = (bf16[64,640]{1,0:T(8,128)(2,1)S(1)}, bf16[64,640]{1,0:T(8,128)(2,1)S(1)}, u32[]{:S(2)}, u32[]{:S(2)}) collective-permute-start(bf16[64,640]{1,0:T(8,128)(2,1)S(1)} %pack_lists.6), channel_id=1, source_target_pairs={{0,24},{8,16},{16,8},{24,0},{1,25},{9,17},{17,9},{25,1},{2,26},{10... | collective-permute-start | bytes 245768 | tf_op jit(solution)/shard_map/ppermute | solution.py:585
  58.1 4.7 %collective-permute-start.6 = (bf16[64,640]{1,0:T(8,128)(2,1)S(1)}, bf16[64,640]{1,0:T(8,128)(2,1)S(1)}, u32[]{:S(2)}, u32[]{:S(2)}) collective-permute-start(bf16[64,640]{1,0:T(8,128)(2,1)S(1)} %get-tuple-element.97), channel_id=1, source_target_pairs={{0,8},{8,0},{16,24},{24,16},{1,9},{9,1},{17,25},{25,17},{2,10},{10... | collective-permute-start | bytes 245768 | tf_op jit(solution)/shard_map/ppermute | solution.py:585
  58.7 4.4 %collective-permute-start.7 = (bf16[64,640]{1,0:T(8,128)(2,1)S(1)}, bf16[64,640]{1,0:T(8,128)(2,1)S(1)}, u32[]{:S(2)}, u32[]{:S(2)}) collective-permute-start(bf16[64,640]{1,0:T(8,128)(2,1)S(1)} %get-tuple-element.98), channel_id=1, source_target_pairs={{0,16},{8,24},{16,0},{24,8},{1,17},{9,25},{17,1},{25,9},{2,18},{10... | collective-permute-start | bytes 245768 | tf_op jit(solution)/shard_map/ppermute | solution.py:585
where the time goes:
time: 67.6 us; the launch traced here: 67.2 us
  Pallas kernels  28.5 us (42%)
  starting transfers between devices  20.5 us (30%)
  waiting for transfers between devices  15.3 us (23%)
  between operations  1.48 us (2%)
  local copies, waits for them, and re-layouts  0.74 us (1%)
  other arithmetic  0.7 us (1%)
    all_to_all x3, starting transfers between devices, exchange(): return lax.all_to_all(value, axis, split_axis=0, concat_axis=0, tiled=True)  13.4 us
    all_to_all x3, waiting for transfers between devices, exchange(): return lax.all_to_all(value, axis, split_axis=0, concat_axis=0, tiled=True)  11.6 us
    ppermute x6, starting transfers between devices, swap(): return lax.ppermute(value, axis, [(i, i ^ distance) for i in range(size)])  7.11 us
    pallas_call x1, Pallas kernels, plan_turn(): pl.pallas_call(functools.partial(plan_kernel, own), out_shape=[jax.ShapeD...  6.94 us
    pallas_call x1, Pallas kernels, gather_columns(): pl.pallas_call(gather_kernel, out_shape=[jax.ShapeDtypeStruct(shape, tabl...  6.81 us
    pallas_call x1, Pallas kernels, run_layer(): pl.pallas_call(layer_kernel, out_shape=[shape, shape], in_specs=[smem, sm...  6.62 us
    pallas_call x3, Pallas kernels, pack_lists(): pl.pallas_call(functools.partial(pack_kernel, distances), out_shape=[jax....  4.12 us
    pallas_call x1, Pallas kernels, scatter_slots(): pl.pallas_call(functools.partial(scatter_kernel, groups, stack), grid=(ow...  4.03 us
  transfers between devices with their start and end apart: 9, of which 7 were waited for; matrix products, arithmetic and copies ran while one was open for 2% of the time, Pallas kernels for 16%

commit v1 on v0

--- a/solution.py
+++ b/solution.py
@@ -34,7 +34,7 @@
 BLOCK = 256
 UNROLL = 128
 AT_ONCE = 32
-CHUNKS = 4
+CHUNKS = 8
 
 
 def gather_kernel(
@@ -442,7 +442,10 @@
         rank = rank_ref[pl.ds((groups + owner) * users, users), :]
         fits = (ids_ref[0] >> own_bits == owner) & (rank >= 0) & (rank < capacity)
         slot = jnp.where(fits, rank + owner * capacity, slot)
-    slot_ref[...] = slot
+    padded = jnp.concatenate(
+        [slot.astype(F32), jnp.zeros((LANES - users, positions), F32)], axis=0
+    )
+    slot_ref[...] = padded.T.astype(jnp.int32)
 
     digit = lax.broadcasted_iota(jnp.int32, (LOW, positions), 0)
     place = lax.broadcasted_iota(jnp.int32, (capacity, positions), 0)
@@ -478,7 +481,7 @@
         out_shape=[
             jax.ShapeDtypeStruct((groups, capacity, LOW), BF16),
             jax.ShapeDtypeStruct((groups, capacity), F32),
-            jax.ShapeDtypeStruct((users, positions), jnp.int32),
+            jax.ShapeDtypeStruct((positions, LANES), jnp.int32),
             jax.ShapeDtypeStruct((1,), jnp.int32),
         ],
         in_specs=[smem, smem, vmem],
@@ -499,10 +502,6 @@
     *packed_refs, wide_ref, chosen_ref = refs
     users, _, positions = grad_ref.shape
     capacity = packed_refs[0].shape[1]
-    padded = jnp.concatenate(
-        [slot_ref[...].astype(F32), jnp.zeros((LANES - users, positions), F32)], axis=0
-    )
-    slots = padded.T.astype(jnp.int32)
     place = lax.broadcasted_iota(jnp.int32, (positions, capacity), 1)
     for user in range(users):
         wide_ref[:, pl.ds(user * positions, positions)] = grad_ref[user]
@@ -510,7 +509,7 @@
         first = (home_ref[0] ^ distance) * capacity
         for user in range(users):
             chosen_ref[pl.ds(user * positions, positions), :] = jnp.where(
-                place == slots[:, user : user + 1] - first, 1.0, 0.0
+                place == slot_ref[:, user : user + 1] - first, 1.0, 0.0
             ).astype(BF16)
         packed_ref[...] = dot_nn(wide_ref[...], chosen_ref[...]).astype(BF16)
 

time: 67.6 us -> 67.5 us (level)
  no operation moved by 1% of the time
where the time goes in v1:
time: 67.5 us; the launch traced here: 67.1 us
  Pallas kernels  28.4 us (42%)
  starting transfers between devices  20.5 us (30%)
  waiting for transfers between devices  15.3 us (23%)
  between operations  1.48 us (2%)
  local copies, waits for them, and re-layouts  0.74 us (1%)
  other arithmetic  0.7 us (1%)
    all_to_all x3, starting transfers between devices, exchange(): return lax.all_to_all(value, axis, split_axis=0, concat_axis=0, tiled=True)  13.4 us
    all_to_all x3, waiting for transfers between devices, exchange(): return lax.all_to_all(value, axis, split_axis=0, concat_axis=0, tiled=True)  11.8 us
    ppermute x6, starting transfers between devices, swap(): return lax.ppermute(value, axis, [(i, i ^ distance) for i in range(size)])  7.11 us
    pallas_call x1, Pallas kernels, plan_turn(): pl.pallas_call(functools.partial(plan_kernel, own), out_shape=[jax.ShapeD...  7.05 us
    pallas_call x1, Pallas kernels, gather_columns(): pl.pallas_call(gather_kernel, out_shape=[jax.ShapeDtypeStruct(shape, tabl...  6.89 us
    pallas_call x1, Pallas kernels, run_layer(): pl.pallas_call(layer_kernel, out_shape=[shape, shape], in_specs=[smem, sm...  6.62 us
    pallas_call x1, Pallas kernels, scatter_slots(): pl.pallas_call(functools.partial(scatter_kernel, groups, stack), grid=(ow...  4.03 us
    pallas_call x3, Pallas kernels, pack_lists(): pl.pallas_call(functools.partial(pack_kernel, distances), out_shape=[jax....  3.81 us
  transfers between devices with their start and end apart: 9, of which 7 were waited for; matrix products, arithmetic and copies ran while one was open for 2% of the time, Pallas kernels for 16%

profile of v1, /device:TPU:0, one launch (start us, length us, event | category | flops | bytes accessed | tf_op | source)
XLA Modules:
  0.0 67.1 jit_solution(11944142379259890509)
XLA Ops:
  0.6 0.0 copy-start.4
  0.6 0.0 copy-start.3
  0.7 0.0 copy-start.2
  0.7 0.0 copy-start.1
  0.7 0.0 copy-start
  0.7 6.9 %gather_columns.1 = (bf16[8,128,256]{2,1,0:T(8,128)(2,1)}, s32[8,256]{1,0:T(8,128)}) custom-call(s32[8]{0:T(128)} %len_ref.3, s32[2048]{0:T(1024)} %ids_ref.1, bf16[64,2048]{1,0:T(8,128)(2,1)} %cot_hbm_ref.1, bf16[64,32768]{1,0:T(8,128)(2,1)} %table_hbm_ref.1), custom_call_target="tpu_custom_call" | custom-call | flops 8000000000 | bytes 5000000 | tf_op jit(solution)/shard_map/gather_columns/pallas_call | solution.py:151
  7.6 6.3 %all-to-all-start = ((bf16[8,128,256]{2,1,0:T(8,128)(2,1)}), bf16[8,128,256]{2,1,0:T(8,128)(2,1)S(1)}, u32[]{:S(2)}, u32[]{:S(2)}) async-start(bf16[8,128,256]{2,1,0:T(8,128)(2,1)} %get-tuple-element.77), calls=%async_computation | async-start | bytes 1048576 | tf_op jit(solution)/shard_map/all_to_all | solution.py:598
  13.9 2.4 %collective-permute-start.5 = (s32[8,256]{1,0:T(8,128)}, s32[8,256]{1,0:T(8,128)S(1)}, u32[]{:S(2)}, u32[]{:S(2)}) collective-permute-start(s32[8,256]{1,0:T(8,128)} %get-tuple-element.79), channel_id=1, source_target_pairs={{0,24},{8,16},{16,8},{24,0},{1,25},{9,17},{17,9},{25,1},{2,26},{10... | collective-permute-start | bytes 24584 | tf_op jit(solution)/shard_map/ppermute | solution.py:584
  16.4 0.5 collective-permute-start.4
  16.9 0.5 collective-permute-start.3
  17.4 1.3 %collective-permute-done.5 = s32[8,256]{1,0:T(8,128)S(1)} collective-permute-done((s32[8,256]{1,0:T(8,128)}, s32[8,256]{1,0:T(8,128)S(1)}, u32[]{:S(2)}, u32[]{:S(2)}) %collective-permute-start.5) | collective-permute-done | bytes 8224 | tf_op jit(solution)/shard_map/ppermute | solution.py:584
  18.7 1.5 %collective-permute-done.4 = s32[8,256]{1,0:T(8,128)S(1)} collective-permute-done((s32[8,256]{1,0:T(8,128)}, s32[8,256]{1,0:T(8,128)S(1)}, u32[]{:S(2)}, u32[]{:S(2)}) %collective-permute-start.4) | collective-permute-done | bytes 8224 | tf_op jit(solution)/shard_map/ppermute | solution.py:584
  20.2 0.5 collective-permute-done.3
  20.7 0.7 %pad_add_fusion.ids_ref = s32[4,8,256]{2,1,0:T(8,128)S(1)} fusion(s32[1,8,256]{2,1,0:T(8,128)S(1)} %bitcast.25, s32[1,8,256]{2,1,0:T(8,128)S(1)} %bitcast.26, s32[1,8,256]{2,1,0:T(8,128)S(1)} %bitcast.27, s32[1,8,256]{2,1,0:T(8,128)} %bitcast.24), kind=kLoop, calls=%fused_computation | loop fusion | flops 24576 | bytes 65536 | tf_op jit(solution)/shard_map/stack | solution.py:617
  21.4 7.8 %all-to-all-done.recv_ref = bf16[8,128,256]{2,1,0:T(8,128)(2,1)S(1)} async-done(((bf16[8,128,256]{2,1,0:T(8,128)(2,1)}), bf16[8,128,256]{2,1,0:T(8,128)(2,1)S(1)}, u32[]{:S(2)}, u32[]{:S(2)}) %all-to-all-start) | async-done | bytes 524320 | tf_op jit(solution)/shard_map/all_to_all | solution.py:598
  29.3 0.0 copy-done.4
  29.3 0.0 copy-done.3
  29.3 0.0 copy-done.2
  29.3 0.0 copy-done.1
  29.3 0.0 copy-done
  29.3 6.6 %layer.1 = (bf16[512,256]{1,0:T(8,128)(2,1)}, bf16[512,256]{1,0:T(8,128)(2,1)}) custom-call(s32[1]{0:T(128)} %bitcast.2.me_ref, s32[8]{0:T(128)S(1)} %copy-done.4, bf16[8,128,256]{2,1,0:T(8,128)(2,1)S(1)} %all-to-all-done.recv_ref, bf16[512,2048]{1,0:T(8,128)(2,1)S(1)} %copy-done, bf16[512,512]{1,0:T(8,128)(2,1)S(1)} %copy-done.1, f32[512]{0:T(512)S(1)} %copy-done.2, ...), custom_call_target="tpu_custom_call" | custom-call | flops 10000000000 | bytes 10000000 | tf_op jit(solution)/shard_map/layer/pallas_call | solution.py:375
  35.9 3.4 %all-to-all-start.1 = ((bf16[8,64,256]{2,1,0:T(8,128)(2,1)}), bf16[8,64,256]{2,1,0:T(8,128)(2,1)S(1)}, u32[]{:S(2)}, u32[]{:S(2)}) async-start(bf16[8,64,256]{2,1,0:T(8,128)(2,1)} %bitcast.7), calls=%async_computation.1 | async-start | bytes 524288 | tf_op jit(solution)/shard_map/all_to_all | solution.py:598
  39.4 7.0 %plan_turn.2 = (bf16[4,640,256]{2,1,0:T(8,128)(2,1)S(1)}, f32[4,640]{1,0:T(4,128)S(1)}, s32[256,128]{1,0:T(8,128)S(1)}, s32[1]{0:T(128)}) custom-call(s32[1]{0:T(128)} %bitcast.8.home_ref, s32[1]{0:T(128)} %constant.26.clone.1.turn_ref, s32[4,8,256]{2,1,0:T(8,128)S(1)} %pad_add_fusion.ids_ref), custom_call_target="tpu_custom_call" | custom-call | flops 4000000000 | bytes 5000000 | tf_op jit(solution)/shard_map/plan_turn/pallas_call | solution.py:479
  46.4 2.6 %all-to-all-done.1.grad_ref = bf16[8,64,256]{2,1,0:T(8,128)(2,1)S(1)} async-done(((bf16[8,64,256]{2,1,0:T(8,128)(2,1)}), bf16[8,64,256]{2,1,0:T(8,128)(2,1)S(1)}, u32[]{:S(2)}, u32[]{:S(2)}) %all-to-all-start.1) | async-done | bytes 262176 | tf_op jit(solution)/shard_map/all_to_all | solution.py:598
  49.0 3.6 %all-to-all-start.2 = ((bf16[8,64,256]{2,1,0:T(8,128)(2,1)}), bf16[8,64,256]{2,1,0:T(8,128)(2,1)S(1)}, u32[]{:S(2)}, u32[]{:S(2)}) async-start(bf16[8,64,256]{2,1,0:T(8,128)(2,1)} %bitcast.9), calls=%async_computation.2 | async-start | bytes 524288 | tf_op jit(solution)/shard_map/all_to_all | solution.py:598
  52.6 1.0 %pack_lists.6 = bf16[64,640]{1,0:T(8,128)(2,1)S(1)} custom-call(s32[1]{0:T(128)} %bitcast.8.home_ref, s32[256,128]{1,0:T(8,128)S(1)} %get-tuple-element.92.slot_ref, bf16[8,64,256]{2,1,0:T(8,128)(2,1)S(1)} %all-to-all-done.1.grad_ref), custom_call_target="tpu_custom_call" | custom-call | flops 800000000 | bytes 1000000 | tf_op jit(solution)/shard_map/pack_lists/pallas_call | solution.py:520
  53.6 2.5 %collective-permute-start.8 = (bf16[64,640]{1,0:T(8,128)(2,1)S(1)}, bf16[64,640]{1,0:T(8,128)(2,1)S(1)}, u32[]{:S(2)}, u32[]{:S(2)}) collective-permute-start(bf16[64,640]{1,0:T(8,128)(2,1)S(1)} %pack_lists.6), channel_id=1, source_target_pairs={{0,24},{8,16},{16,8},{24,0},{1,25},{9,17},{17,9},{25,1},{2,26},{10... | collective-permute-start | bytes 245768 | tf_op jit(solution)/shard_map/ppermute | solution.py:584
  56.2 1.8 %pack_lists.7 = (bf16[64,640]{1,0:T(8,128)(2,1)S(1)}, bf16[64,640]{1,0:T(8,128)(2,1)S(1)}) custom-call(s32[1]{0:T(128)} %bitcast.8.home_ref, s32[256,128]{1,0:T(8,128)S(1)} %get-tuple-element.92.slot_ref, bf16[8,64,256]{2,1,0:T(8,128)(2,1)S(1)} %all-to-all-done.1.grad_ref), custom_call_target="tpu_custom_call" | custom-call | flops 1600000000 | bytes 1000000 | tf_op jit(solution)/shard_map/pack_lists/pallas_call | solution.py:520
  58.0 0.6 collective-permute-start.6
  58.6 0.5 collective-permute-start.7
  59.8 1.0 %pack_lists.8.refs_0_ = bf16[64,640]{1,0:T(8,128)(2,1)S(1)} custom-call(s32[1]{0:T(128)} %bitcast.8.home_ref, s32[256,128]{1,0:T(8,128)S(1)} %get-tuple-element.92.slot_ref, bf16[8,64,256]{2,1,0:T(8,128)(2,1)S(1)} %all-to-all-done.1.grad_ref), custom_call_target="tpu_custom_call" | custom-call | flops 800000000 | bytes 1000000 | tf_op jit(solution)/shard_map/pack_lists/pallas_call | solution.py:520
  60.8 1.3 %all-to-all-done.2 = bf16[8,64,256]{2,1,0:T(8,128)(2,1)S(1)} async-done(((bf16[8,64,256]{2,1,0:T(8,128)(2,1)}), bf16[8,64,256]{2,1,0:T(8,128)(2,1)S(1)}, u32[]{:S(2)}, u32[]{:S(2)}) %all-to-all-start.2) | async-done | bytes 262176 | tf_op jit(solution)/shard_map/all_to_all | solution.py:598
  62.1 0.7 %copy.12 = bf16[8,8,8,256]{3,2,0,1:T(8,128)(2,1)} copy(bf16[8,8,8,256]{3,2,1,0:T(8,128)(2,1)S(1)} %bitcast.22) | data formatting | bytes 524288 | tf_op jit(solution)/shard_map/reshape | solution.py:629
  62.8 0.0 collective-permute-done.8.refs_3_
  62.8 0.0 collective-permute-done.6.refs_1_
  62.8 0.2 collective-permute-done.7.refs_2_
  63.0 4.0 %scatter_slots.2 = f32[64,8192]{1,0:T(8,128)} custom-call(bf16[2560,256]{1,0:T(8,128)(2,1)S(1)} %bitcast.20, f32[4,640]{1,0:T(4,128)S(1)} %get-tuple-element.102.high_ref, bf16[64,640]{1,0:T(8,128)(2,1)S(1)} %pack_lists.8.refs_0_, bf16[64,640]{1,0:T(8,128)(2,1)S(1)} %collective-permute-done.6.refs_1_, bf16[64,640]{1,0:T(8,128)(2,1)S(1)} %collective-permute-done.7.refs_2_, ...), custom_call_target="tpu_custom_call" | custom-call | flops 3000000000 | bytes 1000000 | tf_op jit(solution)/shard_map/scatter_slots/pallas_call | solution.py:563
  (1 shorter events, 0.0 us)
Async XLA Ops:
  0.6 28.7 %copy-start.4 = (s32[8]{0:T(128)S(1)}, s32[8]{0:T(128)}, u32[]{:S(2)}) copy-start(s32[8]{0:T(128)} %len_ref.3) | copy-start | bytes 100
  0.6 28.6 %copy-start.3 = (f32[512]{0:T(512)S(1)}, f32[512]{0:T(512)}, u32[]{:S(2)}) copy-start(f32[512]{0:T(512)} %gain_mid_row_ref.1) | copy-start | bytes 6148
  0.7 28.6 %copy-start.2 = (f32[512]{0:T(512)S(1)}, f32[512]{0:T(512)}, u32[]{:S(2)}) copy-start(f32[512]{0:T(512)} %gain_in_row_ref.1) | copy-start | bytes 6148
  0.7 28.6 %copy-start.1 = (bf16[512,512]{1,0:T(8,128)(2,1)S(1)}, bf16[512,512]{1,0:T(8,128)(2,1)}, u32[]{:S(2)}) copy-start(bf16[512,512]{1,0:T(8,128)(2,1)} %w_out_ref.1) | copy-start | bytes 1572868
  0.7 28.6 %copy-start = (bf16[512,2048]{1,0:T(8,128)(2,1)S(1)}, bf16[512,2048]{1,0:T(8,128)(2,1)}, u32[]{:S(2)}) copy-start(bf16[512,2048]{1,0:T(8,128)(2,1)} %w_in_ref.1) | copy-start | bytes 6291460
  7.6 21.7 %all-to-all-start = ((bf16[8,128,256]{2,1,0:T(8,128)(2,1)}), bf16[8,128,256]{2,1,0:T(8,128)(2,1)S(1)}, u32[]{:S(2)}, u32[]{:S(2)}) async-start(bf16[8,128,256]{2,1,0:T(8,128)(2,1)} %get-tuple-element.77), calls=%async_computation | async-start | bytes 1048576 | tf_op jit(solution)/shard_map/all_to_all | solution.py:598
  13.9 4.8 %collective-permute-start.5 = (s32[8,256]{1,0:T(8,128)}, s32[8,256]{1,0:T(8,128)S(1)}, u32[]{:S(2)}, u32[]{:S(2)}) collective-permute-start(s32[8,256]{1,0:T(8,128)} %get-tuple-element.79), channel_id=1, source_target_pairs={{0,24},{8,16},{16,8},{24,0},{1,25},{9,17},{17,9},{25,1},{2,26},{10... | collective-permute-start | bytes 24584 | tf_op jit(solution)/shard_map/ppermute | solution.py:584
  16.4 3.9 %collective-permute-start.4 = (s32[8,256]{1,0:T(8,128)}, s32[8,256]{1,0:T(8,128)S(1)}, u32[]{:S(2)}, u32[]{:S(2)}) collective-permute-start(s32[8,256]{1,0:T(8,128)} %get-tuple-element.79), channel_id=1, source_target_pairs={{0,16},{8,24},{16,0},{24,8},{1,17},{9,25},{17,1},{25,9},{2,18},{10... | collective-permute-start | bytes 24584 | tf_op jit(solution)/shard_map/ppermute | solution.py:584
  16.9 3.9 %collective-permute-start.3 = (s32[8,256]{1,0:T(8,128)}, s32[8,256]{1,0:T(8,128)S(1)}, u32[]{:S(2)}, u32[]{:S(2)}) collective-permute-start(s32[8,256]{1,0:T(8,128)} %get-tuple-element.79), channel_id=1, source_target_pairs={{0,8},{8,0},{16,24},{24,16},{1,9},{9,1},{17,25},{25,17},{2,10},{10... | collective-permute-start | bytes 24584 | tf_op jit(solution)/shard_map/ppermute | solution.py:584
  35.9 13.1 %all-to-all-start.1 = ((bf16[8,64,256]{2,1,0:T(8,128)(2,1)}), bf16[8,64,256]{2,1,0:T(8,128)(2,1)S(1)}, u32[]{:S(2)}, u32[]{:S(2)}) async-start(bf16[8,64,256]{2,1,0:T(8,128)(2,1)} %bitcast.7), calls=%async_computation.1 | async-start | bytes 524288 | tf_op jit(solution)/shard_map/all_to_all | solution.py:598
  49.0 13.1 %all-to-all-start.2 = ((bf16[8,64,256]{2,1,0:T(8,128)(2,1)}), bf16[8,64,256]{2,1,0:T(8,128)(2,1)S(1)}, u32[]{:S(2)}, u32[]{:S(2)}) async-start(bf16[8,64,256]{2,1,0:T(8,128)(2,1)} %bitcast.9), calls=%async_computation.2 | async-start | bytes 524288 | tf_op jit(solution)/shard_map/all_to_all | solution.py:598
  53.6 9.2 %collective-permute-start.8 = (bf16[64,640]{1,0:T(8,128)(2,1)S(1)}, bf16[64,640]{1,0:T(8,128)(2,1)S(1)}, u32[]{:S(2)}, u32[]{:S(2)}) collective-permute-start(bf16[64,640]{1,0:T(8,128)(2,1)S(1)} %pack_lists.6), channel_id=1, source_target_pairs={{0,24},{8,16},{16,8},{24,0},{1,25},{9,17},{17,9},{25,1},{2,26},{10... | collective-permute-start | bytes 245768 | tf_op jit(solution)/shard_map/ppermute | solution.py:584
  58.0 4.9 %collective-permute-start.6 = (bf16[64,640]{1,0:T(8,128)(2,1)S(1)}, bf16[64,640]{1,0:T(8,128)(2,1)S(1)}, u32[]{:S(2)}, u32[]{:S(2)}) collective-permute-start(bf16[64,640]{1,0:T(8,128)(2,1)S(1)} %get-tuple-element.97), channel_id=1, source_target_pairs={{0,8},{8,0},{16,24},{24,16},{1,9},{9,1},{17,25},{25,17},{2,10},{10... | collective-permute-start | bytes 245768 | tf_op jit(solution)/shard_map/ppermute | solution.py:584
  58.6 4.4 %collective-permute-start.7 = (bf16[64,640]{1,0:T(8,128)(2,1)S(1)}, bf16[64,640]{1,0:T(8,128)(2,1)S(1)}, u32[]{:S(2)}, u32[]{:S(2)}) collective-permute-start(bf16[64,640]{1,0:T(8,128)(2,1)S(1)} %get-tuple-element.98), channel_id=1, source_target_pairs={{0,16},{8,24},{16,0},{24,8},{1,17},{9,25},{17,1},{25,9},{2,18},{10... | collective-permute-start | bytes 245768 | tf_op jit(solution)/shard_map/ppermute | solution.py:584
